TPU v7x, 32 devices: a whole 2x2x4 slice. The times are simulated.
32 devices in a mesh: row: 4 (over z), col: 8 (over y, x, core).
Axes of the slice: x: 2, y: 2, z: 4, core: 2. Of those that a mesh axis runs over, the one named last changes fastest.
Arguments:
- sources: float32 [30, 4096], P(None, ('row', 'col')), may hold values from -12 to 12
- log_source_mass: float32 [4096], P(('row', 'col')), may hold values from -4 to 4
- targets: float32 [30, 4096], P(None, 'col'), may hold values from -6 to 6
- log_target_mass: float32 [4096], P('col'), may hold values from -4 to 4
- start_potential: float32 [4096], P('col'), may hold values from -12 to 250
Outputs:
- row_potential: float32 [4096], P(('row', 'col'))
- column_potential: float32 [4096], P('col')
All inputs are finite; a program needn't handle non-finite values.
Results may differ from a plain program's by a relative error of at most 0.00015.
Values sent between devices are 32-bit elements; how exact they have to be, the bound alone decides.
A program may use at most 64 MiB of HBM per device.

v0:
```python
import math

import jax
import jax.numpy as jnp
from jax import lax
from jax.sharding import PartitionSpec as P

ITERS = 2


entropic_scale = 2.0
lowest = -1e30
block_width = 2048


def tile_scores(own_coords, own_sq, other):
    dims = own_coords.shape[0]
    coords = other[:dims]
    inner = lax.dot_general(
        own_coords,
        coords,
        (((0,), (0,)), ((), ())),
        precision=lax.Precision.HIGHEST,
        preferred_element_type=jnp.float32,
    )
    other_sq = 0.5 * jnp.sum(coords * coords, axis=0)
    cost = own_sq[:, None] + other_sq[None, :] - inner
    return other[dims][None, :] - cost / entropic_scale


def merge_pair(first, second):
    peak = jnp.maximum(first[0], second[0])
    return (peak, first[1] * jnp.exp(first[0] - peak) + second[1] * jnp.exp(second[0] - peak))


def online_fold(own_coords, partial_value, piece):
    own_sq = 0.5 * jnp.sum(own_coords * own_coords, axis=0)
    length = piece.shape[1]
    width = math.gcd(length, block_width)
    blocks = piece.reshape(piece.shape[0], length // width, width).transpose(1, 0, 2)

    def advance(running, block):
        scores = tile_scores(own_coords, own_sq, block)
        block_max = jnp.max(scores, axis=1)
        block_sum = jnp.sum(jnp.exp(scores - block_max[:, None]), axis=1)
        return (merge_pair(running, (block_max, block_sum)), None)

    result, unused = lax.scan(advance, partial_value, blocks)
    return result


def on_device(sources, log_source_mass, targets, log_target_mass, start_potential):
    own_rows = sources.shape[1]
    own_cols = targets.shape[1]
    target_term = start_potential / entropic_scale + log_target_mass
    row_potential = jnp.zeros((own_rows,), jnp.float32)
    column_potential = start_potential
    for sweep in range(ITERS):
        target_pack = jnp.concatenate([targets, target_term[None, :]], axis=0)
        row_start = (
            jnp.full((own_rows,), lowest, jnp.float32),
            jnp.zeros((own_rows,), jnp.float32),
        )
        row_peak, row_total = online_fold(
            sources, row_start, lax.all_gather(target_pack, "col", axis=1, tiled=True)
        )
        row_potential = -entropic_scale * (row_peak + jnp.log(row_total))
        source_term = row_potential / entropic_scale + log_source_mass
        source_pack = jnp.concatenate([sources, source_term[None, :]], axis=0)
        col_start = (
            jnp.full((own_cols,), lowest, jnp.float32),
            jnp.zeros((own_cols,), jnp.float32),
        )
        col_peak, col_total = online_fold(
            targets, col_start, lax.all_gather(source_pack, "col", axis=1, tiled=True)
        )
        overall = lax.pmax(col_peak, "row")
        col_total = lax.psum(col_total * jnp.exp(col_peak - overall), "row")
        col_peak = overall
        column_potential = -entropic_scale * (col_peak + jnp.log(col_total))
        target_term = column_potential / entropic_scale + log_target_mass
    return (row_potential, column_potential)


def solution(mesh):
    return jax.shard_map(
        on_device,
        mesh=mesh,
        in_specs=(P(None, ("row", "col")), P(("row", "col")), P(None, "col"), P("col"), P("col")),
        out_specs=(P(("row", "col")), P("col")),
        check_vma=False,
    )
```

profile of v0, /device:TPU:0, one launch (start us, length us, event | category | flops | bytes accessed | tf_op | source)
XLA Modules:
  0.0 102.4 jit_solution(5988775618188881214)
XLA Ops:
  0.6 0.7 multiply_reduce_fusion.5
  1.4 0.7 multiply_add_fusion.1
  2.1 0.8 pad_maximum_fusion
  2.9 11.3 %all_gather.12 = f32[31,4096]{1,0:T(8,128)S(1)} all-gather(f32[31,512]{1,0:T(8,128)S(1)} %pad_maximum_fusion), channel_id=1, replica_groups=mesh['row'=4,'col'=8] {'col'}, dimensions={1}, use_global_device_ids=true | all-gather | bytes 571392 | tf_op jit(solution)/shard_map/all_gather | solution.py:65
  14.2 0.4 reshape.43
  14.7 7.4 %while.6 = (s32[]{:T(128)}, f32[128]{0:T(128)S(1)}, f32[128]{0:T(128)S(1)}, f32[2,31,2048]{2,0,1:T(2,128)S(1)}, f32[128]{0:T(128)S(1)}, /*index=5*/f32[30,128]{1,0:T(8,128)}, s32[]{:T(128)}, s32[]{:T(128)}, s32[]{}) while((s32[]{:T(128)}, f32[128]{0:T(128)S(1)}, f32[128]{0:T(128)S(1)}, f32[2,31,2048]{2,0,1:T(2,128)S(1)}, ...), condition=%wide.region_5.6_spmd.clone, body=%wide.region_1.5_spmd.clone.sunk | while | flops 96330496 | bytes 3158143 | solution.py:48
  14.7 0.3 constant_dynamic-slice_fusion.8
  15.1 3.0 %fusion.35 = (f32[128]{0:T(128)S(1)}, f32[128,2048]{0,1:T(8,128)S(1)}) fusion(f32[30,128]{1,0:T(8,128)} %get-tuple-element.313, f32[1,30,2048]{2,0,1:T(1,128)S(1)} %constant_dynamic-slice_fusion.8, f32[2048]{0:T(1024)S(1)} %broadcast_multiply_fusion.9, f32[128]{0:T(128)S(1)} %get-tuple-element.312, f32[2048]{0:T(1024)S(1)} %bitcast.80), kind=kOutput, calls=%fused_computation.63.clone.1 | convolution fusion | flops 95682432 | bytes 1327104 | tf_op jit(solution)/shard_map/while/body/eval_jaxpr/dot_general | solution.py:19
  18.1 0.3 exponential_reduce_fusion.6
  18.4 0.3 constant_dynamic-slice_fusion.8
  18.8 3.0 %fusion.35 = (f32[128]{0:T(128)S(1)}, f32[128,2048]{0,1:T(8,128)S(1)}) fusion(f32[30,128]{1,0:T(8,128)} %get-tuple-element.313, f32[1,30,2048]{2,0,1:T(1,128)S(1)} %constant_dynamic-slice_fusion.8, f32[2048]{0:T(1024)S(1)} %broadcast_multiply_fusion.9, f32[128]{0:T(128)S(1)} %get-tuple-element.312, f32[2048]{0:T(1024)S(1)} %bitcast.80), kind=kOutput, calls=%fused_computation.63.clone.1 | convolution fusion | flops 95682432 | bytes 1327104 | tf_op jit(solution)/shard_map/while/body/eval_jaxpr/dot_general | solution.py:19
  21.8 0.3 exponential_reduce_fusion.6
  22.2 0.7 pad_maximum_fusion.2
  22.9 9.3 %all_gather.13 = f32[31,1024]{1,0:T(8,128)S(1)} all-gather(f32[31,128]{1,0:T(8,128)S(1)} %pad_maximum_fusion.2), channel_id=1, replica_groups=mesh['row'=4,'col'=8] {'col'}, dimensions={1}, use_global_device_ids=true | all-gather | bytes 142848 | tf_op jit(solution)/shard_map/all_gather | solution.py:75
  32.3 2.1 %fusion.22 = (f32[512]{0:T(512)S(1)}, f32[512,1024]{0,1:T(8,128)S(1)}) fusion(f32[30,512]{1,0:T(8,128)S(1)} %copy-done, f32[31,1024]{1,0:T(8,128)S(1)} %all_gather.13, f32[1024]{0:T(1024)S(1)} %broadcast_multiply_fusion.3, f32[512]{0:T(512)S(1)} %broadcast_multiply_fusion.4, f32[1024]{0:T(1024)S(1)} %bitcast.84), kind=kOutput, calls=%fused_computation.65 | convolution fusion | flops 191364608 | bytes 2297856 | tf_op jit(solution)/shard_map/while/body/eval_jaxpr/dot_general | solution.py:19
  34.4 0.4 exponential_reduce_fusion.3
  34.8 12.0 %pmax.14 = f32[512]{0:T(512)S(1)} all-reduce(f32[512]{0:T(512)S(1)} %broadcast_maximum_fusion.1), channel_id=1, replica_groups=mesh['row'=4,'col'=8] {'row'}, use_global_device_ids=true, to_apply=%region_9.10 | all-reduce | flops 512 | bytes 4096 | tf_op jit(solution)/shard_map/pmax | solution.py:77
  46.8 8.4 %psum.14 = f32[512]{0:T(512)S(1)} all-reduce(f32[512]{0:T(512)S(1)} %exponential_multiply_fusion.1), channel_id=1, replica_groups=mesh['row'=4,'col'=8] {'row'}, use_global_device_ids=true, to_apply=%region_11.12 | all-reduce | flops 512 | bytes 4096 | tf_op jit(solution)/shard_map/psum | solution.py:78
  55.1 8.9 %all_gather.14 = f32[31,4096]{1,0:T(8,128)S(1)} all-gather(f32[31,512]{1,0:T(8,128)S(1)} %pad_maximum_fusion.1), channel_id=1, replica_groups=mesh['row'=4,'col'=8] {'col'}, dimensions={1}, use_global_device_ids=true | all-gather | bytes 571392 | tf_op jit(solution)/shard_map/all_gather | solution.py:65
  64.0 0.4 reshape.44
  64.5 6.0 %while.7 = (s32[]{:T(128)}, f32[128]{0:T(128)S(1)}, f32[128]{0:T(128)S(1)}, f32[2,31,2048]{2,0,1:T(2,128)S(1)}, f32[128]{0:T(128)S(1)}, /*index=5*/f32[30,128]{1,0:T(8,128)S(1)}, s32[]{:T(128)}, s32[]{:T(128)}, s32[]{}) while((s32[]{:T(128)}, f32[128]{0:T(128)S(1)}, f32[128]{0:T(128)S(1)}, f32[2,31,2048]{2,0,1:T(2,128)S(1)}, ...), condition=%wide.region_16.17_spmd.clone, body=%wide.region_12.16_spmd.clone.sunk | while | flops 96330496 | bytes 3158143 | solution.py:48
  64.9 2.3 %fusion.38 = (f32[128]{0:T(128)S(1)}, f32[128,2048]{0,1:T(8,128)S(1)}) fusion(f32[30,128]{1,0:T(8,128)S(1)} %get-tuple-element.340, f32[1,30,2048]{2,0,1:T(1,128)S(1)} %constant_dynamic-slice_fusion.10, f32[2048]{0:T(1024)S(1)} %broadcast_multiply_fusion.10, f32[128]{0:T(128)S(1)} %get-tuple-element.339, f32[2048]{0:T(1024)S(1)} %bitcast.81), kind=kOutput, calls=%fused_computation.64.clone.1 | convolution fusion | flops 95682432 | bytes 1327104 | tf_op jit(solution)/shard_map/while/body/eval_jaxpr/dot_general | solution.py:19
  67.2 0.3 exponential_reduce_fusion.7
  67.9 2.3 %fusion.38 = (f32[128]{0:T(128)S(1)}, f32[128,2048]{0,1:T(8,128)S(1)}) fusion(f32[30,128]{1,0:T(8,128)S(1)} %get-tuple-element.340, f32[1,30,2048]{2,0,1:T(1,128)S(1)} %constant_dynamic-slice_fusion.10, f32[2048]{0:T(1024)S(1)} %broadcast_multiply_fusion.10, f32[128]{0:T(128)S(1)} %get-tuple-element.339, f32[2048]{0:T(1024)S(1)} %bitcast.81), kind=kOutput, calls=%fused_computation.64.clone.1 | convolution fusion | flops 95682432 | bytes 1327104 | tf_op jit(solution)/shard_map/while/body/eval_jaxpr/dot_general | solution.py:19
  70.2 0.3 exponential_reduce_fusion.7
  70.5 0.5 add_bitcast_fusion
  71.0 9.4 %all_gather.15 = f32[31,1024]{1,0:T(8,128)S(1)} all-gather(f32[31,128]{1,0:T(8,128)S(1)} %pad_maximum_fusion.3), channel_id=1, replica_groups=mesh['row'=4,'col'=8] {'col'}, dimensions={1}, use_global_device_ids=true | all-gather | bytes 142848 | tf_op jit(solution)/shard_map/all_gather | solution.py:75
  80.5 2.1 %fusion.23 = (f32[512]{0:T(512)S(1)}, f32[512,1024]{0,1:T(8,128)S(1)}) fusion(f32[30,512]{1,0:T(8,128)S(1)} %copy-done, f32[31,1024]{1,0:T(8,128)S(1)} %all_gather.15, f32[1024]{0:T(1024)S(1)} %broadcast_multiply_fusion.2, f32[512]{0:T(512)S(1)} %broadcast_multiply_fusion.4, f32[1024]{0:T(1024)S(1)} %bitcast.85), kind=kOutput, calls=%fused_computation.66 | convolution fusion | flops 191364608 | bytes 2297856 | tf_op jit(solution)/shard_map/while/body/eval_jaxpr/dot_general | solution.py:19
  82.6 0.4 exponential_reduce_fusion.2
  83.0 10.4 %pmax.15 = f32[512]{0:T(512)S(1)} all-reduce(f32[512]{0:T(512)S(1)} %broadcast_maximum_fusion), channel_id=1, replica_groups=mesh['row'=4,'col'=8] {'row'}, use_global_device_ids=true, to_apply=%region_19.20 | all-reduce | flops 512 | bytes 4096 | tf_op jit(solution)/shard_map/pmax | solution.py:77
  93.4 8.4 %psum.15 = f32[512]{0:T(512)S(1)} all-reduce(f32[512]{0:T(512)S(1)} %exponential_multiply_fusion), channel_id=1, replica_groups=mesh['row'=4,'col'=8] {'row'}, use_global_device_ids=true, to_apply=%region_21.22 | all-reduce | flops 512 | bytes 4096 | tf_op jit(solution)/shard_map/psum | solution.py:78
  101.8 0.6 add_multiply_fusion
  (47 shorter events, 1.2 us)
Async XLA Ops:
  14.7 7.5 %copy-start.3 = (f32[128]{0:T(128)S(1)}, f32[128]{0:T(128)}, u32[]{:S(2)}) copy-start(f32[128]{0:T(128)} %param.10) | copy-start | bytes 1540
  14.7 17.5 %copy-start = (f32[30,512]{1,0:T(8,128)S(1)}, f32[30,512]{1,0:T(8,128)}, u32[]{:S(2)}) copy-start(f32[30,512]{1,0:T(8,128)} %param.11) | copy-start | bytes 184324
  32.3 22.9 %copy-start.2 = (f32[512]{0:T(512)S(1)}, f32[512]{0:T(512)}, u32[]{:S(2)}) copy-start(f32[512]{0:T(512)} %param.12) | copy-start | bytes 6148
  34.4 30.1 %copy-start.1 = (f32[30,128]{1,0:T(8,128)S(1)}, f32[30,128]{1,0:T(8,128)}, u32[]{:S(2)}) copy-start(f32[30,128]{1,0:T(8,128)} %get-tuple-element.344) | copy-start | bytes 46084
where the time goes:
time: 103 us; the launch traced here: 102 us
  blocking collectives  78 us (76%)
  matrix products  14.8 us (14%)
  other arithmetic  6.64 us (6%)
  local copies, waits for them, and re-layouts  1.98 us (2%)
    pmax x2, blocking collectives, on_device(): overall = lax.pmax(col_peak, 'row')  22.3 us
    all_gather x2, blocking collectives, on_device(): lax.all_gather(target_pack, 'col', axis=1, tiled=True)  20.2 us
    all_gather x2, blocking collectives, on_device(): lax.all_gather(source_pack, 'col', axis=1, tiled=True)  18.7 us
    psum x2, blocking collectives, on_device(): col_total = lax.psum(col_total * jnp.exp(col_peak - overall), 'row')  16.7 us
    dot_general x6, matrix products, tile_scores(): lax.dot_general(own_coords, coords, (((0,), (0,)), ((), ())), precision=l...  14.8 us

commit v1 on v0

v1 whole, which is shorter than its diff:
```python
import functools

import jax
import jax.numpy as jnp
from jax import lax
from jax.experimental import pallas as pl
from jax.experimental.pallas import tpu as pltpu
from jax.sharding import PartitionSpec as P

ITERS = 2
MESH = pl.DeviceIdType.MESH
LANES = 128
EXTRA = 16
LOG2E = 1.4426950408889634
LN2 = 0.6931471805599453


def split3(x):
    hi = x.astype(jnp.bfloat16).astype(jnp.float32)
    rest = x - hi
    mid = rest.astype(jnp.bfloat16).astype(jnp.float32)
    return hi, mid, rest - mid


def term_rows(term):
    hi, mid, low = split3(term)
    row = lax.broadcasted_iota(jnp.int32, (EXTRA, term.shape[1]), 0)
    zero = jnp.zeros((EXTRA, term.shape[1]), jnp.float32)
    return jnp.where(row == 0, hi, jnp.where(row == 1, mid, jnp.where(row == 2, low, zero))).astype(jnp.bfloat16)


def one_rows(n):
    row = lax.broadcasted_iota(jnp.int32, (EXTRA, n), 0)
    return jnp.where(row < 3, 1.0, 0.0).astype(jnp.bfloat16)


def merge(parts):
    peak = parts[0]
    for part in parts[1:]:
        peak = jnp.maximum(peak, part)
    total = jnp.exp2(parts[0] - peak)
    for part in parts[1:]:
        total = total + jnp.exp2(part - peak)
    return peak + jnp.log2(total)


def column_lse(left, right, lo, hi, out, slot):
    width = right.shape[1]
    step = 256 if width % 256 == 0 else LANES
    for at in range(0, width, step):
        scores = lax.dot_general(
            left[lo:hi, :],
            right[lo:hi, at : at + step],
            (((0,), (0,)), ((), ())),
            preferred_element_type=jnp.float32,
        )
        peak = jnp.max(scores, axis=0, keepdims=True)
        total = jnp.sum(jnp.exp2(scores - peak), axis=0, keepdims=True)
        part = peak + jnp.log2(total)
        for k in range(step // LANES):
            b = at // LANES + k
            out[slot, b : b + 1, :] = part[:, k * LANES : (k + 1) * LANES]


def kernel(
    nr, nc, src, lsm, tgt, ltm, pot, row_out, col_out,
    gathered, left, right, lsm2, row_lse, row_parts, col_parts,
    gather_send, gather_recv, row_send, row_recv, col_send, col_recv,
):
    r, c = lax.axis_index("row"), lax.axis_index("col")
    dims, own = src.shape
    height = gathered.shape[1]
    cols = tgt.shape[1]
    row_blocks, col_blocks = nc * own // LANES, cols // LANES
    per = own // LANES

    barrier = pltpu.get_barrier_semaphore()
    for d in range(1, nc):
        pl.semaphore_signal(barrier, inc=1, device_id=(r, lax.rem(c + d, nc)), device_id_type=MESH)
    for d in range(1, nr):
        pl.semaphore_signal(barrier, inc=1, device_id=(lax.rem(r + d, nr), c), device_id_type=MESH)

    gathered[c, 0:dims, :] = src[...]
    for q in range(per):
        gathered[c, dims : dims + 1, q * LANES : (q + 1) * LANES] = lsm[q : q + 1, :]
    gathered[c, dims + 1 : height, :] = jnp.zeros((height - dims - 1, own), jnp.float32)

    pl.semaphore_wait(barrier, nc + nr - 2)

    def along_col(buf, send, recv, d):
        return pltpu.make_async_remote_copy(
            src_ref=buf.at[c], dst_ref=buf.at[c], send_sem=send.at[d - 1], recv_sem=recv.at[d - 1],
            device_id=(r, lax.rem(c + d, nc)), device_id_type=MESH,
        )

    def along_row(buf, send, recv, d):
        return pltpu.make_async_remote_copy(
            src_ref=buf.at[r], dst_ref=buf.at[r], send_sem=send.at[d - 1], recv_sem=recv.at[d - 1],
            device_id=(lax.rem(r + d, nr), c), device_id_type=MESH,
        )

    copies = [along_col(gathered, gather_send, gather_recv, d) for d in range(1, nc)]
    for copy in copies:
        copy.start()

    lead = EXTRA
    tail = EXTRA + 6 * height
    coords = jnp.concatenate([tgt[...], jnp.zeros((height - dims, cols), jnp.float32)], axis=0)
    t1, t2, t3 = [part.astype(jnp.bfloat16) for part in split3(coords)]
    for k, part in enumerate((t1, t1, t2, t2, t1, t3)):
        left[lead + k * height : lead + (k + 1) * height, :] = part
    left[tail : tail + EXTRA, :] = one_rows(cols)
    target_sq = jnp.sum(coords * coords, axis=0, keepdims=True)
    for b in range(col_blocks):
        at = slice(b * LANES, (b + 1) * LANES)
        term = (0.5 * pot[b : b + 1, :] + ltm[b : b + 1, :]) * LOG2E - (0.25 * LOG2E) * target_sq[:, at]
        left[0:EXTRA, at] = term_rows(term)
    right[0:EXTRA, :] = one_rows(nc * own)

    for copy in copies:
        copy.wait()

    for k in range(nc):
        at = slice(k * own, (k + 1) * own)
        block = gathered[k]
        for q in range(per):
            b = k * per + q
            lsm2[b : b + 1, :] = block[dims : dims + 1, q * LANES : (q + 1) * LANES] * LOG2E
        s1, s2, s3 = [part.astype(jnp.bfloat16) for part in split3(block * (0.5 * LOG2E))]
        for g, part in enumerate((s1, s2, s1, s2, s3, s1)):
            right[lead + g * height : lead + (g + 1) * height, at] = part

    for sweep in range(ITERS):
        parts = row_parts.at[sweep]
        column_lse(left, right, 0, tail, parts, c)
        copies = [along_col(parts, row_send.at[sweep], row_recv.at[sweep], d) for d in range(1, nc)]
        for copy in copies:
            copy.start()
        for copy in copies:
            copy.wait()
        lse = merge([parts[k] for k in range(nc)])
        if sweep == ITERS - 1:
            row_lse[...] = lse
        term = lsm2[...] - lse
        for b in range(row_blocks):
            right[tail : tail + EXTRA, b * LANES : (b + 1) * LANES] = term_rows(term[b : b + 1, :])

        parts = col_parts.at[sweep]
        column_lse(right, left, lead, tail + EXTRA, parts, r)
        copies = [along_row(parts, col_send.at[sweep], col_recv.at[sweep], d) for d in range(1, nr)]
        for copy in copies:
            copy.start()
        if sweep == ITERS - 1:
            own_sq = jnp.sum(src[...] * src[...], axis=0, keepdims=True)
            for q in range(per):
                row_out[q : q + 1, :] = (
                    0.5 * own_sq[:, q * LANES : (q + 1) * LANES]
                    - (2.0 * LN2) * row_lse[pl.ds(c * per + q, 1), :]
                )
        for copy in copies:
            copy.wait()
        lse = merge([parts[k] for k in range(nr)])
        if sweep < ITERS - 1:
            term = ltm[...] * LOG2E - lse
            for b in range(col_blocks):
                left[0:EXTRA, b * LANES : (b + 1) * LANES] = term_rows(term[b : b + 1, :])
        else:
            for b in range(col_blocks):
                at = slice(b * LANES, (b + 1) * LANES)
                col_out[b : b + 1, :] = 0.5 * target_sq[:, at] - (2.0 * LN2) * lse[b : b + 1, :]


def on_device(nr, nc, sources, log_source_mass, targets, log_target_mass, start_potential):
    dims, own = sources.shape
    cols = targets.shape[1]
    height = -(-(dims + 2) // EXTRA) * EXTRA
    deep = 6 * height + 2 * EXTRA
    row_blocks, col_blocks = nc * own // LANES, cols // LANES
    vmem = pl.BlockSpec(memory_space=pltpu.VMEM)
    row, col = pl.pallas_call(
        functools.partial(kernel, nr, nc),
        out_shape=(
            jax.ShapeDtypeStruct((own // LANES, LANES), jnp.float32),
            jax.ShapeDtypeStruct((col_blocks, LANES), jnp.float32),
        ),
        in_specs=[vmem] * 5,
        out_specs=(vmem, vmem),
        scratch_shapes=[
            pltpu.VMEM((nc, height, own), jnp.float32),
            pltpu.VMEM((deep, cols), jnp.bfloat16),
            pltpu.VMEM((deep, nc * own), jnp.bfloat16),
            pltpu.VMEM((row_blocks, LANES), jnp.float32),
            pltpu.VMEM((row_blocks, LANES), jnp.float32),
            pltpu.VMEM((ITERS, nc, row_blocks, LANES), jnp.float32),
            pltpu.VMEM((ITERS, nr, col_blocks, LANES), jnp.float32),
            pltpu.SemaphoreType.DMA((nc - 1,)),
            pltpu.SemaphoreType.DMA((nc - 1,)),
            pltpu.SemaphoreType.DMA((ITERS, nc - 1)),
            pltpu.SemaphoreType.DMA((ITERS, nc - 1)),
            pltpu.SemaphoreType.DMA((ITERS, nr - 1)),
            pltpu.SemaphoreType.DMA((ITERS, nr - 1)),
        ],
        compiler_params=pltpu.CompilerParams(
            collective_id=0, has_side_effects=True, vmem_limit_bytes=48 * 1024 * 1024
        ),
    )(
        sources,
        log_source_mass.reshape(own // LANES, LANES),
        targets,
        log_target_mass.reshape(col_blocks, LANES),
        start_potential.reshape(col_blocks, LANES),
    )
    return row.reshape(own), col.reshape(cols)


def solution(mesh):
    return jax.shard_map(
        functools.partial(on_device, mesh.shape["row"], mesh.shape["col"]),
        mesh=mesh,
        in_specs=(P(None, ("row", "col")), P(("row", "col")), P(None, "col"), P("col"), P("col")),
        out_specs=(P(("row", "col")), P("col")),
        check_vma=False,
    )
```

time: 103 us -> 30.5 us (0.30)
  blocking collectives: 78 us -> 0 us
  Pallas kernels: 0 us -> 26.3 us
  matrix products: 14.8 us -> 0 us
  other arithmetic: 6.64 us -> 0 us
  local copies, waits for them, and re-layouts: 1.98 us -> 3.32 us
    all_gather x4 -> x0, blocking collectives: 38.9 us -> none  [the longest x2 20.2 us: on_device(): lax.all_gather(target_pack, 'col', axis=1, tiled=True)]
    pallas_call x0 -> x1, Pallas kernels: none -> 26.3 us  [on_device(): pl.pallas_call(functools.partial(kernel, nr, nc), out_shape=(jax.ShapeDty...]
    pmax x2 -> x0, blocking collectives: 22.3 us -> none  [on_device(): overall = lax.pmax(col_peak, 'row')]
    psum x2 -> x0, blocking collectives: 16.7 us -> none  [on_device(): col_total = lax.psum(col_total * jnp.exp(col_peak - overall), 'row')]
    dot_general x6 -> x0, matrix products: 14.8 us -> none  [tile_scores(): lax.dot_general(own_coords, coords, (((0,), (0,)), ((), ())), precision=l...]
    unnamed x8 -> x12, local copies, waits for them, and re-layouts: 0.03 us -> 3.32 us
    reduce_sum x14 -> x0, other arithmetic: 3.06 us -> none  [the longest x6 1.9 us: advance(): block_sum = jnp.sum(jnp.exp(scores - block_max[:, None]), axis=1)]
    concatenate x4 -> x0, other arithmetic: 1.6 us -> none  [the longest x2 0.86 us: on_device(): target_pack = jnp.concatenate([targets, target_term[None, :]], axis=0)]
where the time goes in v1:
time: 30.5 us; the launch traced here: 30.3 us
  Pallas kernels  26.3 us (86%)
  local copies, waits for them, and re-layouts  3.32 us (11%)
  between operations  0.67 us (2%)
    pallas_call x1, Pallas kernels, on_device(): pl.pallas_call(functools.partial(kernel, nr, nc), out_shape=(jax.ShapeDty...  26.3 us
    unnamed x12, local copies, waits for them, and re-layouts  3.32 us

profile of v1, /device:TPU:0, one launch (start us, length us, event | category | flops | bytes accessed | tf_op | source)
XLA Modules:
  0.0 30.3 jit_solution(5824875628909599349)
XLA Ops:
  0.6 0.0 copy-start.3
  0.6 0.0 copy-start.2
  0.7 0.0 copy-start.4
  0.7 0.7 %copy-done.3 = f32[512]{0:T(512)S(1)} copy-done((f32[512]{0:T(512)S(1)}, f32[512]{0:T(512)}, u32[]{:S(2)}) %copy-start.3) | copy-done | bytes 2072
  1.3 0.0 copy-done.2
  1.3 0.0 copy-done.4
  1.3 0.0 copy-start
  1.3 0.8 %copy-done = f32[30,512]{1,0:T(8,128)S(1)} copy-done((f32[30,512]{1,0:T(8,128)S(1)}, f32[30,512]{1,0:T(8,128)}, u32[]{:S(2)}) %copy-start) | copy-done | bytes 61464
  2.2 0.0 copy-start.1
  2.2 0.7 %copy-done.1 = f32[30,128]{1,0:T(8,128)S(1)} copy-done((f32[30,128]{1,0:T(8,128)S(1)}, f32[30,128]{1,0:T(8,128)}, u32[]{:S(2)}) %copy-start.1) | copy-done | bytes 15384
  2.9 26.3 %shard_map.68 = (f32[1,128]{1,0:T(1,128)S(1)}, f32[4,128]{1,0:T(4,128)S(1)}) custom-call(f32[30,128]{1,0:T(8,128)S(1)} %copy-done.1, f32[1,128]{1,0:T(1,128)S(1)} %bitcast.8, f32[30,512]{1,0:T(8,128)S(1)} %copy-done, f32[4,128]{1,0:T(4,128)S(1)} %bitcast.5, f32[4,128]{1,0:T(4,128)S(1)} %bitcast.6), custom_call_target="tpu_custom_call" | custom-call | tf_op jit(solution)/shard_map/pallas_call | solution.py:180
  29.2 0.5 %copy.9 = f32[128]{0:T(128)} copy(f32[128]{0:T(128)S(1)} %bitcast.9) | data formatting | bytes 1024
  29.7 0.6 %copy.10 = f32[512]{0:T(512)} copy(f32[512]{0:T(512)S(1)} %bitcast.7) | data formatting | bytes 4096
Async XLA Ops:
  0.6 0.7 %copy-start.3 = (f32[512]{0:T(512)S(1)}, f32[512]{0:T(512)}, u32[]{:S(2)}) copy-start(f32[512]{0:T(512)} %param.9) | copy-start | bytes 6148
  0.6 0.7 %copy-start.2 = (f32[512]{0:T(512)S(1)}, f32[512]{0:T(512)}, u32[]{:S(2)}) copy-start(f32[512]{0:T(512)} %param.8) | copy-start | bytes 6148
  0.7 0.7 %copy-start.4 = (f32[128]{0:T(128)S(1)}, f32[128]{0:T(128)}, u32[]{:S(2)}) copy-start(f32[128]{0:T(128)} %param.6) | copy-start | bytes 1540
  1.3 0.8 %copy-start = (f32[30,512]{1,0:T(8,128)S(1)}, f32[30,512]{1,0:T(8,128)}, u32[]{:S(2)}) copy-start(f32[30,512]{1,0:T(8,128)} %tgt.1) | copy-start | bytes 184324
  2.2 0.7 %copy-start.1 = (f32[30,128]{1,0:T(8,128)S(1)}, f32[30,128]{1,0:T(8,128)}, u32[]{:S(2)}) copy-start(f32[30,128]{1,0:T(8,128)} %src.1) | copy-start | bytes 46084

commit v2 on v1

--- a/solution.py
+++ b/solution.py
@@ -63,23 +63,33 @@
 
 
 def kernel(
-    nr, nc, src, lsm, tgt, ltm, pot, row_out, col_out,
-    gathered, left, right, lsm2, row_lse, row_parts, col_parts,
+    nr, nc, src_in, lsm_in, tgt_in, ltm_in, pot_in, row_out, col_out,
+    src, lsm, tgt, ltm, pot, load_sem, gathered, left, right, lsm2, row_lse, row_parts, col_parts,
     gather_send, gather_recv, row_send, row_recv, col_send, col_recv,
 ):
     r, c = lax.axis_index("row"), lax.axis_index("col")
+    barrier = pltpu.get_barrier_semaphore()
+    for d in range(1, nc):
+        pl.semaphore_signal(barrier, inc=1, device_id=(r, lax.rem(c + d, nc)), device_id_type=MESH)
+    for d in range(1, nr):
+        pl.semaphore_signal(barrier, inc=1, device_id=(lax.rem(r + d, nr), c), device_id_type=MESH)
+
+    loads = [
+        pltpu.make_async_copy(here, there, load_sem.at[k])
+        for k, (here, there) in enumerate(
+            ((src_in, src), (lsm_in, lsm), (tgt_in, tgt), (ltm_in, ltm), (pot_in, pot))
+        )
+    ]
+    for load in loads:
+        load.start()
     dims, own = src.shape
     height = gathered.shape[1]
     cols = tgt.shape[1]
     row_blocks, col_blocks = nc * own // LANES, cols // LANES
     per = own // LANES
 
-    barrier = pltpu.get_barrier_semaphore()
-    for d in range(1, nc):
-        pl.semaphore_signal(barrier, inc=1, device_id=(r, lax.rem(c + d, nc)), device_id_type=MESH)
-    for d in range(1, nr):
-        pl.semaphore_signal(barrier, inc=1, device_id=(lax.rem(r + d, nr), c), device_id_type=MESH)
-
+    loads[0].wait()
+    loads[1].wait()
     gathered[c, 0:dims, :] = src[...]
     for q in range(per):
         gathered[c, dims : dims + 1, q * LANES : (q + 1) * LANES] = lsm[q : q + 1, :]
@@ -102,6 +112,9 @@
     copies = [along_col(gathered, gather_send, gather_recv, d) for d in range(1, nc)]
     for copy in copies:
         copy.start()
+
+    for load in loads[2:]:
+        load.wait()
 
     lead = EXTRA
     tail = EXTRA + 6 * height
@@ -118,7 +131,7 @@
     right[0:EXTRA, :] = one_rows(nc * own)
 
     for copy in copies:
-        copy.wait()
+        copy.wait_recv()
 
     for k in range(nc):
         at = slice(k * own, (k + 1) * own)
@@ -130,6 +143,7 @@
         for g, part in enumerate((s1, s2, s1, s2, s3, s1)):
             right[lead + g * height : lead + (g + 1) * height, at] = part
 
+    sent = copies
     for sweep in range(ITERS):
         parts = row_parts.at[sweep]
         column_lse(left, right, 0, tail, parts, c)
@@ -137,7 +151,8 @@
         for copy in copies:
             copy.start()
         for copy in copies:
-            copy.wait()
+            copy.wait_recv()
+        sent += copies
         lse = merge([parts[k] for k in range(nc)])
         if sweep == ITERS - 1:
             row_lse[...] = lse
@@ -158,7 +173,8 @@
                     - (2.0 * LN2) * row_lse[pl.ds(c * per + q, 1), :]
                 )
         for copy in copies:
-            copy.wait()
+            copy.wait_recv()
+        sent += copies
         lse = merge([parts[k] for k in range(nr)])
         if sweep < ITERS - 1:
             term = ltm[...] * LOG2E - lse
@@ -168,6 +184,8 @@
             for b in range(col_blocks):
                 at = slice(b * LANES, (b + 1) * LANES)
                 col_out[b : b + 1, :] = 0.5 * target_sq[:, at] - (2.0 * LN2) * lse[b : b + 1, :]
+    for copy in sent:
+        copy.wait_send()
 
 
 def on_device(nr, nc, sources, log_source_mass, targets, log_target_mass, start_potential):
@@ -183,9 +201,15 @@
             jax.ShapeDtypeStruct((own // LANES, LANES), jnp.float32),
             jax.ShapeDtypeStruct((col_blocks, LANES), jnp.float32),
         ),
-        in_specs=[vmem] * 5,
+        in_specs=[pl.BlockSpec(memory_space=pltpu.HBM)] * 5,
         out_specs=(vmem, vmem),
         scratch_shapes=[
+            pltpu.VMEM((dims, own), jnp.float32),
+            pltpu.VMEM((own // LANES, LANES), jnp.float32),
+            pltpu.VMEM((dims, cols), jnp.float32),
+            pltpu.VMEM((col_blocks, LANES), jnp.float32),
+            pltpu.VMEM((col_blocks, LANES), jnp.float32),
+            pltpu.SemaphoreType.DMA((5,)),
             pltpu.VMEM((nc, height, own), jnp.float32),
             pltpu.VMEM((deep, cols), jnp.bfloat16),
             pltpu.VMEM((deep, nc * own), jnp.bfloat16),
@@ -204,13 +228,17 @@
             collective_id=0, has_side_effects=True, vmem_limit_bytes=48 * 1024 * 1024
         ),
     )(
-        sources,
-        log_source_mass.reshape(own // LANES, LANES),
-        targets,
-        log_target_mass.reshape(col_blocks, LANES),
-        start_potential.reshape(col_blocks, LANES),
+        hbm(sources),
+        hbm(log_source_mass.reshape(own // LANES, LANES)),
+        hbm(targets),
+        hbm(log_target_mass.reshape(col_blocks, LANES)),
+        hbm(start_potential.reshape(col_blocks, LANES)),
     )
     return row.reshape(own), col.reshape(cols)
+
+
+def hbm(x):
+    return pltpu.with_memory_space_constraint(x, pltpu.HBM)
 
 
 def solution(mesh):

time: 30.5 us -> 28.4 us (0.931)
  local copies, waits for them, and re-layouts: 3.32 us -> 1.09 us
    unnamed x12 -> x2, local copies, waits for them, and re-layouts: 3.32 us -> 1.09 us
where the time goes in v2:
time: 28.4 us; the launch traced here: 28.1 us
  Pallas kernels  26.4 us (93%)
  local copies, waits for them, and re-layouts  1.09 us (4%)
  between operations  0.64 us (2%)
    pallas_call x1, Pallas kernels, on_device(): pl.pallas_call(functools.partial(kernel, nr, nc), out_shape=(jax.ShapeDty...  26.4 us
    unnamed x2, local copies, waits for them, and re-layouts  1.09 us

profile of v2, /device:TPU:0, one launch (start us, length us, event | category | flops | bytes accessed | tf_op | source)
XLA Modules:
  0.0 28.1 jit_solution(5227562289553394884)
XLA Ops:
  0.6 26.4 %shard_map.68 = (f32[1,128]{1,0:T(1,128)S(1)}, f32[4,128]{1,0:T(4,128)S(1)}) custom-call(f32[30,128]{1,0:T(8,128)} %src_in.1, f32[1,128]{1,0:T(1,128)} %bitcast.9, f32[30,512]{1,0:T(8,128)} %tgt_in.1, f32[4,128]{1,0:T(4,128)} %bitcast.7, f32[4,128]{1,0:T(4,128)} %bitcast.8), custom_call_target="tpu_custom_call" | custom-call | tf_op jit(solution)/shard_map/pallas_call | solution.py:198
  27.0 0.5 %copy.9 = f32[128]{0:T(128)} copy(f32[128]{0:T(128)S(1)} %bitcast.6) | data formatting | bytes 1024
  27.6 0.6 %copy.10 = f32[512]{0:T(512)} copy(f32[512]{0:T(512)S(1)} %bitcast.5) | data formatting | bytes 4096

commit v3 on v2

--- a/solution.py
+++ b/solution.py
@@ -13,6 +13,8 @@
 EXTRA = 16
 LOG2E = 1.4426950408889634
 LN2 = 0.6931471805599453
+LEFT = (0, 0, 1, 1, 0, 2)
+RIGHT = (0, 1, 0, 1, 2, 0)
 
 
 def split3(x):
@@ -26,7 +28,7 @@
     hi, mid, low = split3(term)
     row = lax.broadcasted_iota(jnp.int32, (EXTRA, term.shape[1]), 0)
     zero = jnp.zeros((EXTRA, term.shape[1]), jnp.float32)
-    return jnp.where(row == 0, hi, jnp.where(row == 1, mid, jnp.where(row == 2, low, zero))).astype(jnp.bfloat16)
+    return jnp.where(row == 0, hi, jnp.where(row == 1, mid, jnp.where(row == 2, low, zero)))
 
 
 def one_rows(n):
@@ -44,16 +46,11 @@
     return peak + jnp.log2(total)
 
 
-def column_lse(left, right, lo, hi, out, slot):
+def column_lse(left_t, right, out, slot):
     width = right.shape[1]
     step = 256 if width % 256 == 0 else LANES
     for at in range(0, width, step):
-        scores = lax.dot_general(
-            left[lo:hi, :],
-            right[lo:hi, at : at + step],
-            (((0,), (0,)), ((), ())),
-            preferred_element_type=jnp.float32,
-        )
+        scores = jnp.dot(left_t[...], right[:, at : at + step], preferred_element_type=jnp.float32)
         peak = jnp.max(scores, axis=0, keepdims=True)
         total = jnp.sum(jnp.exp2(scores - peak), axis=0, keepdims=True)
         part = peak + jnp.log2(total)
@@ -62,9 +59,26 @@
             out[slot, b : b + 1, :] = part[:, k * LANES : (k + 1) * LANES]
 
 
+def turn_coords(parts, order, out):
+    for b in range(out.shape[0] // LANES):
+        blocks = [part[:, b * LANES : (b + 1) * LANES] for part in parts]
+        at = slice(b * LANES, (b + 1) * LANES)
+        width = 0
+        per = LANES // blocks[0].shape[0]
+        for first in range(0, len(order), per):
+            stack = jnp.concatenate([blocks[k] for k in order[first : first + per]], axis=0)
+            out[at, width : width + stack.shape[0]] = stack.T.astype(jnp.bfloat16)
+            width += stack.shape[0]
+
+
+def turn_term(term, out, tail):
+    for b in range(term.shape[0]):
+        out[b * LANES : (b + 1) * LANES, tail : tail + EXTRA] = term_rows(term[b : b + 1, :]).T.astype(jnp.bfloat16)
+
+
 def kernel(
     nr, nc, src_in, lsm_in, tgt_in, ltm_in, pot_in, row_out, col_out,
-    src, lsm, tgt, ltm, pot, load_sem, gathered, left, right, lsm2, row_lse, row_parts, col_parts,
+    src, lsm, tgt, ltm, pot, load_sem, gathered, left, right, left_t, right_t, lsm2, row_lse, row_parts, col_parts,
     gather_send, gather_recv, row_send, row_recv, col_send, col_recv,
 ):
     r, c = lax.axis_index("row"), lax.axis_index("col")
@@ -116,19 +130,19 @@
     for load in loads[2:]:
         load.wait()
 
-    lead = EXTRA
-    tail = EXTRA + 6 * height
+    tail = 6 * height
     coords = jnp.concatenate([tgt[...], jnp.zeros((height - dims, cols), jnp.float32)], axis=0)
-    t1, t2, t3 = [part.astype(jnp.bfloat16) for part in split3(coords)]
-    for k, part in enumerate((t1, t1, t2, t2, t1, t3)):
-        left[lead + k * height : lead + (k + 1) * height, :] = part
+    pieces = split3(coords)
+    for k, p in enumerate(LEFT):
+        left[k * height : (k + 1) * height, :] = pieces[p].astype(jnp.bfloat16)
     left[tail : tail + EXTRA, :] = one_rows(cols)
+    turn_coords(pieces, LEFT, left_t)
     target_sq = jnp.sum(coords * coords, axis=0, keepdims=True)
-    for b in range(col_blocks):
-        at = slice(b * LANES, (b + 1) * LANES)
-        term = (0.5 * pot[b : b + 1, :] + ltm[b : b + 1, :]) * LOG2E - (0.25 * LOG2E) * target_sq[:, at]
-        left[0:EXTRA, at] = term_rows(term)
-    right[0:EXTRA, :] = one_rows(nc * own)
+    target_sq = jnp.concatenate(
+        [target_sq[:, b * LANES : (b + 1) * LANES] for b in range(col_blocks)], axis=0
+    )
+    turn_term((0.5 * pot[...] + ltm[...]) * LOG2E - (0.25 * LOG2E) * target_sq, left_t, tail)
+    right[tail : tail + EXTRA, :] = one_rows(nc * own)
 
     for copy in copies:
         copy.wait_recv()
@@ -139,29 +153,30 @@
         for q in range(per):
             b = k * per + q
             lsm2[b : b + 1, :] = block[dims : dims + 1, q * LANES : (q + 1) * LANES] * LOG2E
-        s1, s2, s3 = [part.astype(jnp.bfloat16) for part in split3(block * (0.5 * LOG2E))]
-        for g, part in enumerate((s1, s2, s1, s2, s3, s1)):
-            right[lead + g * height : lead + (g + 1) * height, at] = part
+        pieces = split3(block * (0.5 * LOG2E))
+        for g, p in enumerate(RIGHT):
+            right[g * height : (g + 1) * height, at] = pieces[p].astype(jnp.bfloat16)
 
     sent = copies
     for sweep in range(ITERS):
         parts = row_parts.at[sweep]
-        column_lse(left, right, 0, tail, parts, c)
+        column_lse(left_t, right, parts, c)
         copies = [along_col(parts, row_send.at[sweep], row_recv.at[sweep], d) for d in range(1, nc)]
         for copy in copies:
             copy.start()
+        if sweep == 0:
+            for k in range(nc):
+                turn_coords(split3(gathered[k] * (0.5 * LOG2E)), RIGHT, right_t.at[k * own : (k + 1) * own])
         for copy in copies:
             copy.wait_recv()
         sent += copies
         lse = merge([parts[k] for k in range(nc)])
         if sweep == ITERS - 1:
             row_lse[...] = lse
-        term = lsm2[...] - lse
-        for b in range(row_blocks):
-            right[tail : tail + EXTRA, b * LANES : (b + 1) * LANES] = term_rows(term[b : b + 1, :])
+        turn_term(lsm2[...] - lse, right_t, tail)
 
         parts = col_parts.at[sweep]
-        column_lse(right, left, lead, tail + EXTRA, parts, r)
+        column_lse(right_t, left, parts, r)
         copies = [along_row(parts, col_send.at[sweep], col_recv.at[sweep], d) for d in range(1, nr)]
         for copy in copies:
             copy.start()
@@ -177,13 +192,9 @@
         sent += copies
         lse = merge([parts[k] for k in range(nr)])
         if sweep < ITERS - 1:
-            term = ltm[...] * LOG2E - lse
-            for b in range(col_blocks):
-                left[0:EXTRA, b * LANES : (b + 1) * LANES] = term_rows(term[b : b + 1, :])
+            turn_term(ltm[...] * LOG2E - lse, left_t, tail)
         else:
-            for b in range(col_blocks):
-                at = slice(b * LANES, (b + 1) * LANES)
-                col_out[b : b + 1, :] = 0.5 * target_sq[:, at] - (2.0 * LN2) * lse[b : b + 1, :]
+            col_out[...] = 0.5 * target_sq - (2.0 * LN2) * lse
     for copy in sent:
         copy.wait_send()
 
@@ -192,7 +203,7 @@
     dims, own = sources.shape
     cols = targets.shape[1]
     height = -(-(dims + 2) // EXTRA) * EXTRA
-    deep = 6 * height + 2 * EXTRA
+    deep = 6 * height + EXTRA
     row_blocks, col_blocks = nc * own // LANES, cols // LANES
     vmem = pl.BlockSpec(memory_space=pltpu.VMEM)
     row, col = pl.pallas_call(
@@ -213,6 +224,8 @@
             pltpu.VMEM((nc, height, own), jnp.float32),
             pltpu.VMEM((deep, cols), jnp.bfloat16),
             pltpu.VMEM((deep, nc * own), jnp.bfloat16),
+            pltpu.VMEM((cols, deep), jnp.bfloat16),
+            pltpu.VMEM((nc * own, deep), jnp.bfloat16),
             pltpu.VMEM((row_blocks, LANES), jnp.float32),
             pltpu.VMEM((row_blocks, LANES), jnp.float32),
             pltpu.VMEM((ITERS, nc, row_blocks, LANES), jnp.float32),

time: 28.4 us -> 29.4 us (1.035)
  Pallas kernels: 26.4 us -> 27.5 us
    pallas_call x1, Pallas kernels: 26.4 us -> 27.5 us  [on_device(): pl.pallas_call(functools.partial(kernel, nr, nc), out_shape=(jax.ShapeDty...]
where the time goes in v3:
time: 29.4 us; the launch traced here: 29.2 us
  Pallas kernels  27.5 us (94%)
  local copies, waits for them, and re-layouts  1.09 us (4%)
  between operations  0.64 us (2%)
    pallas_call x1, Pallas kernels, on_device(): pl.pallas_call(functools.partial(kernel, nr, nc), out_shape=(jax.ShapeDty...  27.5 us
    unnamed x2, local copies, waits for them, and re-layouts  1.09 us

profile of v3, /device:TPU:0, one launch (start us, length us, event | category | flops | bytes accessed | tf_op | source)
XLA Modules:
  0.0 29.2 jit_solution(14635283060168250706)
XLA Ops:
  0.6 27.5 %shard_map.68 = (f32[1,128]{1,0:T(1,128)S(1)}, f32[4,128]{1,0:T(4,128)S(1)}) custom-call(f32[30,128]{1,0:T(8,128)} %src_in.1, f32[1,128]{1,0:T(1,128)} %bitcast.9, f32[30,512]{1,0:T(8,128)} %tgt_in.1, f32[4,128]{1,0:T(4,128)} %bitcast.7, f32[4,128]{1,0:T(4,128)} %bitcast.8), custom_call_target="tpu_custom_call" | custom-call | tf_op jit(solution)/shard_map/pallas_call | solution.py:209
  28.1 0.5 %copy.9 = f32[128]{0:T(128)} copy(f32[128]{0:T(128)S(1)} %bitcast.6) | data formatting | bytes 1024
  28.6 0.6 %copy.10 = f32[512]{0:T(512)} copy(f32[512]{0:T(512)S(1)} %bitcast.5) | data formatting | bytes 4096
